TPU v7x, 32 devices: a whole 2x2x4 slice. The times are simulated.
32 devices in a mesh: pencil: 32 (over z, y, x, core).
Axes of the slice: x: 2, y: 2, z: 4, core: 2. Of those that a mesh axis runs over, the one named last changes fastest.
Arguments:
- coefficients: float32 [2, 8, 16384, 128], P(None, None, 'pencil'), may hold values from -6 to 6
- potential: float32 [256, 256, 256], P('pencil'), may hold values from -5 to 5
- slot_atom: int32 [2048], P('pencil'), may hold values from 0 to 511, as said below
- slot_count: int32 [32], P('pencil'), may hold values from 8 to 64, as said below
- point_offset: int32 [2048, 256], P('pencil'), may hold values from 0 to 524287
- proj_value: float32 [2048, 8, 256], P('pencil'), may hold values from -0.7 to 0.7
- proj_strength: float32 [512, 8], replicated, may hold values from 0.5 to 4
- proj_count: int32 [512], replicated, may hold values from 1 to 8
Outputs:
- applied_coefficients: float32 [2, 8, 16384, 128], P(None, None, 'pencil')
- projections: float32 [512, 128], P('pencil')
Inputs may be any that keep to these rules, and one draw needn't show every extreme that they name: `slot_atom`: the home block of atom a is a // 16; the atom of every slot of block d has its home block within 2 of d modulo the number of blocks, so (a // 16 - d) modulo the number of blocks is at most 2 or at least the number of blocks minus 2. `slot_count`: some block uses all 64 slots.
All inputs are finite; a program needn't handle non-finite values.
Results may differ from a plain program's by a relative error of at most 0.00011.
Values sent between devices are 32-bit elements; how exact they have to be, the bound alone decides.
A program may use at most 512 MiB of HBM per device.

v0:
```python
import math

import jax
import jax.numpy as jnp
from jax import lax
from jax.sharding import PartitionSpec as P

GRID_SIDE = 256
WAVE_CUTOFF = 128
NPROJ = 8
REACH = 2


def passed_along(block, axis, distance):
    devices = range(lax.axis_size(axis))
    route = [((i - distance) % len(devices), i) for i in devices]
    return lax.ppermute(block, axis, route)


def phase_tables():
    frequency = jnp.arange(WAVE_CUTOFF, dtype=jnp.int32) - WAVE_CUTOFF // 2
    points = jnp.arange(GRID_SIDE, dtype=jnp.int32)
    turn_count = frequency[:, None] * points[None, :] % GRID_SIDE
    phase_angles = 2.0 * math.pi / GRID_SIDE * turn_count.astype(jnp.float32)
    return (jnp.cos(phase_angles), jnp.sin(phase_angles))


def complex_step(real_part, imag_part, full_pattern, table, factor):
    stacked = jnp.stack([real_part, imag_part])
    result = jnp.einsum(full_pattern, stacked, table, precision=lax.Precision.HIGHEST)
    return (factor * result[0], factor * result[1])


def forward_dim(real_part, imag_part, full_pattern, cosine_lookup, sine_lookup, factor):
    table = jnp.stack(
        [jnp.stack([cosine_lookup, sine_lookup]), jnp.stack([-sine_lookup, cosine_lookup])]
    )
    return complex_step(real_part, imag_part, full_pattern, table, factor)


def backward_dim(real_part, imag_part, full_pattern, cosine_lookup, sine_lookup, factor):
    table = jnp.stack(
        [jnp.stack([cosine_lookup, -sine_lookup]), jnp.stack([sine_lookup, cosine_lookup])]
    )
    return complex_step(real_part, imag_part, full_pattern, table, factor)


def columns_to_planes(band_amplitudes, cosine_lookup, sine_lookup):
    real_part, imag_part = forward_dim(
        band_amplitudes[0],
        band_amplitudes[1],
        "rchw,rowa->ocah",
        cosine_lookup,
        sine_lookup,
        WAVE_CUTOFF ** (-0.5),
    )
    return jnp.stack([real_part, imag_part])


def planes_to_grid(incoming_pieces, cosine_lookup, sine_lookup):
    shape_now = incoming_pieces.shape
    real_part = incoming_pieces[0].reshape(shape_now[1], shape_now[2], WAVE_CUTOFF, WAVE_CUTOFF)
    imag_part = incoming_pieces[1].reshape(shape_now[1], shape_now[2], WAVE_CUTOFF, WAVE_CUTOFF)
    real_part, imag_part = forward_dim(
        real_part, imag_part, "rbzkj,rojy->obzky", cosine_lookup, sine_lookup, WAVE_CUTOFF ** (-0.5)
    )
    return forward_dim(
        real_part, imag_part, "rbzky,rokx->obzyx", cosine_lookup, sine_lookup, WAVE_CUTOFF ** (-0.5)
    )


def grid_to_planes(real_part, imag_part, cosine_lookup, sine_lookup):
    real_part, imag_part = backward_dim(
        real_part, imag_part, "rbzyx,rokx->obzyk", cosine_lookup, sine_lookup, GRID_SIDE ** (-0.5)
    )
    real_part, imag_part = backward_dim(
        real_part, imag_part, "rbzyk,rojy->obzkj", cosine_lookup, sine_lookup, GRID_SIDE ** (-0.5)
    )
    shape_now = real_part.shape
    return jnp.stack(
        [
            real_part.reshape(shape_now[0], shape_now[1], WAVE_CUTOFF * WAVE_CUTOFF),
            imag_part.reshape(shape_now[0], shape_now[1], WAVE_CUTOFF * WAVE_CUTOFF),
        ]
    )


def planes_to_columns(incoming_pieces, cosine_lookup, sine_lookup):
    real_part, imag_part = backward_dim(
        incoming_pieces[0],
        incoming_pieces[1],
        "runv,rotn->ouvt",
        cosine_lookup,
        sine_lookup,
        GRID_SIDE ** (-0.5),
    )
    return jnp.stack([real_part, imag_part])


def per_device(
    coefficients,
    potential,
    slot_atom,
    slot_count,
    point_offset,
    proj_value,
    proj_strength,
    proj_count,
):
    highest = lax.Precision.HIGHEST
    cosine_lookup, sine_lookup = phase_tables()
    device = lax.axis_index("pencil")
    devices_all = lax.axis_size("pencil")
    band_total = coefficients.shape[1]
    column_local = coefficients.shape[2]
    incoming_pieces = lax.all_to_all(
        columns_to_planes(coefficients, cosine_lookup, sine_lookup),
        "pencil",
        split_axis=2,
        concat_axis=3,
        tiled=True,
    )
    real_field, imag_field = planes_to_grid(incoming_pieces, cosine_lookup, sine_lookup)
    plane_local = real_field.shape[1]
    field_row_values = 2 * band_total
    fields = jnp.stack([real_field, imag_field]).reshape(
        field_row_values, plane_local * GRID_SIDE * GRID_SIDE
    )
    coeff_width = field_row_values * NPROJ
    slot_local = slot_atom.shape[0]
    used_total = slot_count[0]
    groups_live = (used_total + 7) // 8

    def gather_group(group_index, coeffs):
        first_slot = group_index * 8
        offsets = lax.dynamic_slice_in_dim(point_offset, first_slot, 8, 0)
        values = lax.dynamic_slice_in_dim(proj_value, first_slot, 8, 0)
        live_slot = first_slot + jnp.arange(8, dtype=jnp.int32) < used_total
        picked = fields[:, offsets]
        slot_terms = jnp.einsum("mst,spt->smp", picked, values, precision=highest)
        slot_terms = jnp.where(live_slot[:, None, None], slot_terms, 0.0).reshape(8, coeff_width)
        return lax.dynamic_update_slice_in_dim(coeffs, slot_terms, first_slot, 0)

    coeffs = lax.fori_loop(
        0, groups_live, gather_group, jnp.zeros((slot_local, coeff_width), jnp.float32)
    )
    atom_total = proj_strength.shape[0]
    atom_dev = atom_total // devices_all
    column_proj = jnp.arange(coeff_width, dtype=jnp.int32) % NPROJ
    proj_mask_all = column_proj[None, :] < proj_count[:, None]
    strength_all = jnp.tile(proj_strength, (1, field_row_values))
    window_size = 2 * REACH + 1
    home_block = slot_atom // atom_dev
    relative = (home_block - device + REACH) % devices_all
    window_index = relative * atom_dev + slot_atom % atom_dev
    onehot = (
        window_index[:, None] == jnp.arange(window_size * atom_dev, dtype=jnp.int32)[None, :]
    ).astype(jnp.float32)
    partial_sum = jnp.dot(onehot.T, coeffs, precision=highest).reshape(
        window_size, atom_dev, coeff_width
    )
    mask_home = lax.dynamic_slice_in_dim(proj_mask_all, device * atom_dev, atom_dev, 0)
    strength_home = lax.dynamic_slice_in_dim(strength_all, device * atom_dev, atom_dev, 0)
    totals = partial_sum[REACH]
    for offset in range(-REACH, REACH + 1):
        if offset != 0:
            totals = totals + passed_along(partial_sum[REACH + offset], "pencil", offset)
    becp_home = jnp.where(mask_home, totals, 0.0)
    energy_home = becp_home * strength_home
    pieces = []
    for offset in range(-REACH, REACH + 1):
        if offset == 0:
            pieces.append(energy_home)
        else:
            pieces.append(passed_along(energy_home, "pencil", -offset))
    window = jnp.concatenate(pieces, 0)
    slot_energy = jnp.dot(onehot, window, precision=highest)

    def apply_group(group_index, projected):
        first_slot = group_index * 8
        offsets = lax.dynamic_slice_in_dim(point_offset, first_slot, 8, 0)
        values = lax.dynamic_slice_in_dim(proj_value, first_slot, 8, 0)
        live_slot = first_slot + jnp.arange(8, dtype=jnp.int32) < used_total
        energy = lax.dynamic_slice_in_dim(slot_energy, first_slot, 8, 0).reshape(
            8, field_row_values, NPROJ
        )
        energy = jnp.where(live_slot[:, None, None], energy, 0.0)
        slot_terms = jnp.einsum("smp,spt->mst", energy, values, precision=highest)
        return projected.at[:, offsets].add(slot_terms)

    projected = lax.fori_loop(0, groups_live, apply_group, jnp.zeros_like(fields))
    applied = potential.reshape(1, -1) * fields + projected
    applied = applied.reshape(2, band_total, plane_local, GRID_SIDE, GRID_SIDE)
    incoming_pieces = lax.all_to_all(
        grid_to_planes(applied[0], applied[1], cosine_lookup, sine_lookup),
        "pencil",
        split_axis=3,
        concat_axis=2,
        tiled=True,
    )
    transformed = planes_to_columns(incoming_pieces, cosine_lookup, sine_lookup)
    columns = device * column_local + jnp.arange(column_local, dtype=jnp.int32)
    freq_x = columns // WAVE_CUTOFF - WAVE_CUTOFF // 2
    freq_y = columns % WAVE_CUTOFF - WAVE_CUTOFF // 2
    freq_z = jnp.arange(WAVE_CUTOFF, dtype=jnp.int32) - WAVE_CUTOFF // 2
    squared = (freq_x * freq_x + freq_y * freq_y)[:, None] + (freq_z * freq_z)[None, :]
    kinetic = 6.0 / (WAVE_CUTOFF * WAVE_CUTOFF) * squared.astype(jnp.float32)
    applied_coefficients = transformed + kinetic[None, None] * coefficients
    return (applied_coefficients, becp_home)


def solution(mesh):
    in_specs = (
        P(None, None, "pencil", None),
        P("pencil", None, None),
        P("pencil"),
        P("pencil"),
        P("pencil", None),
        P("pencil", None, None),
        P(),
        P(),
    )
    out_specs = (P(None, None, "pencil", None), P("pencil", None))
    return jax.shard_map(
        per_device, mesh=mesh, in_specs=in_specs, out_specs=out_specs, check_vma=False
    )
```

profile of v0, /device:TPU:0, one launch (start us, length us, event | category | flops | bytes accessed | tf_op | source)
XLA Modules:
  0.0 3341.8 jit_solution(13825746435939101057)
XLA Ops:
  2.1 11.1 fusion.35
  15.8 8.1 copy.78
  23.9 7.6 all-to-all-start
  32.3 185.2 %all-to-all-done = f32[2,8,256,512]{3,1,0,2:T(8,128)} async-done(((f32[2,8,256,512]{3,1,0,2:T(8,128)}), f32[2,8,256,512]{3,1,0,2:T(8,128)}, u32[]{:S(2)}, u32[]{:S(2)}) %all-to-all-start) | async-done | bytes 8388640 | tf_op jit(solution)/shard_map/all_to_all | solution.py:116
  217.5 8.2 copy.148
  230.2 4.8 stack_reshape_squeeze.6
  239.7 17.0 fusion.31
  256.8 6.6 slice_multiply_fusion.5
  263.3 34.6 %convolution_bitcast_fusion = f32[2,8,8,256,256]{3,4,2,1,0:T(8,128)} fusion(f32[1,8,8,128,256]{3,4,2,1,0:T(8,128)} %get-tuple-element.134, f32[1,8,8,128,256]{3,4,2,1,0:T(8,128)} %get-tuple-element.133, f32[1,2,128,256]{2,3,0,1:T(8,128)S(1)} %get-tuple-element.148, f32[1,2,128,256]{2,3,0,1:T(8,128)S(1)} %get-tuple-element.151), kind=kOutput, calls=%fused_computation.33 | convolution fusion | flops 25774129152 | bytes 50855936 | tf_op jit(solution)/shard_map/rbzky,rokx->obzyx/dot_general | solution.py:30
  297.9 17.7 slice_multiply_fusion.1
  315.7 18.3 pad_maximum_fusion
  334.0 32.0 copy.81
  365.9 29.1 reshape.280
  395.1 124.4 %while.20 = (s32[]{:T(128)}, f32[64,128]{1,0:T(8,128)S(1)}, s32[]{:T(128)}, s32[]{:T(128)}, s32[64,256]{1,0:T(8,128)}, /*index=5*/f32[16,524288]{1,0:T(8,128)}, ...) while((s32[]{:T(128)}, f32[64,128]{1,0:T(8,128)S(1)}, s32[]{:T(128)}, ...), condition=%wide.region_1.2_spmd, body=%wide.region_0.1_spmd.sunk | while | flops 3154966 | bytes 544959 | solution.py:144
  396.0 28.4 gather_fusion
  427.0 28.4 gather_fusion
  458.1 28.4 gather_fusion
  489.1 28.4 gather_fusion
  521.0 123.8 %collective-permute-start.1 = (f32[16,128]{1,0:T(8,128)S(1)}, f32[16,128]{1,0:T(8,128)S(1)}, u32[]{:S(2)}, u32[]{:S(2)}) collective-permute-start(f32[16,128]{1,0:T(8,128)S(1)} %get-tuple-element.156), channel_id=1, source_target_pairs={{1,0},{2,1},{3,2},{4,3},{5,4},{6,5},{7,6},{8,7},{9,8},{10,9},{11,1... | collective-permute-start | bytes 24584 | tf_op jit(solution)/shard_map/ppermute | solution.py:17
  646.1 5.3 collective-permute-done.2
  656.2 5.3 collective-permute-start.6
  665.4 81.1 %broadcast_in_dim.47 = f32[16,524288]{0,1:T(8,128)} broadcast(f32[]{:T(128)} %constant.144.clone.1), dimensions={} | broadcast | bytes 33554436 | tf_op jit(solution)/shard_map/broadcast_in_dim | solution.py:191
  746.6 831.1 %while.21 = (s32[]{:T(128)}, f32[16,524288]{0,1:T(8,128)}, s32[]{:T(128)}, s32[64,256]{1,0:T(8,128)}, f32[64,8,256]{2,1,0:T(8,128)}, /*index=5*/s32[]{:T(128)}, ...) while((s32[]{:T(128)}, f32[16,524288]{0,1:T(8,128)}, s32[]{:T(128)}, ...), condition=%wide.region_4.5_spmd, body=%wide.region_2.4_spmd.sunk | while | flops 3210262 | bytes 33861824 | solution.py:191
  755.3 199.0 %scatter_custom_fusion.5 = f32[16,524288]{0,1:T(8,128)} fusion(f32[16,524288]{0,1:T(8,128)} %get-tuple-element.297, s32[2048]{0:T(1024)S(1)} %get-tuple-element.250, f32[2048,16]{1,0:T(8,128)S(1)} %bitcast.162, s32[2048]{0:T(1024)S(1)} %broadcast_clamp_fusion.5), kind=kCustom, calls=%fused_computation.13.clone.1 | custom fusion | flops 32768 | bytes 33554432 | tf_op jit(solution)/shard_map/while/body/scatter-add | solution.py:189
  963.0 199.0 %scatter_custom_fusion.5 = f32[16,524288]{0,1:T(8,128)} fusion(f32[16,524288]{0,1:T(8,128)} %get-tuple-element.297, s32[2048]{0:T(1024)S(1)} %get-tuple-element.250, f32[2048,16]{1,0:T(8,128)S(1)} %bitcast.162, s32[2048]{0:T(1024)S(1)} %broadcast_clamp_fusion.5), kind=kCustom, calls=%fused_computation.13.clone.1 | custom fusion | flops 32768 | bytes 33554432 | tf_op jit(solution)/shard_map/while/body/scatter-add | solution.py:189
  1170.7 199.0 %scatter_custom_fusion.5 = f32[16,524288]{0,1:T(8,128)} fusion(f32[16,524288]{0,1:T(8,128)} %get-tuple-element.297, s32[2048]{0:T(1024)S(1)} %get-tuple-element.250, f32[2048,16]{1,0:T(8,128)S(1)} %bitcast.162, s32[2048]{0:T(1024)S(1)} %broadcast_clamp_fusion.5), kind=kCustom, calls=%fused_computation.13.clone.1 | custom fusion | flops 32768 | bytes 33554432 | tf_op jit(solution)/shard_map/while/body/scatter-add | solution.py:189
  1378.5 199.0 %scatter_custom_fusion.5 = f32[16,524288]{0,1:T(8,128)} fusion(f32[16,524288]{0,1:T(8,128)} %get-tuple-element.297, s32[2048]{0:T(1024)S(1)} %get-tuple-element.250, f32[2048,16]{1,0:T(8,128)S(1)} %bitcast.162, s32[2048]{0:T(1024)S(1)} %broadcast_clamp_fusion.5), kind=kCustom, calls=%fused_computation.13.clone.1 | custom fusion | flops 32768 | bytes 33554432 | tf_op jit(solution)/shard_map/while/body/scatter-add | solution.py:189
  1577.7 139.1 %copy.83 = f32[16,524288]{1,0:T(8,128)} copy(f32[16,524288]{0,1:T(8,128)} %get-tuple-element.79) | data formatting | bytes 67108864 | tf_op jit(solution)/shard_map/while | solution.py:191
  1716.8 33.5 %multiply_add_fusion = f32[16,524288]{1,0:T(8,128)} fusion(f32[16,524288]{1,0:T(8,128)} %copy.83, f32[16,524288]{1,0:T(8,128)} %get-tuple-element.318, f32[524288]{0:T(1024)S(1)} %bitcast.166), kind=kLoop, calls=%fused_computation.32 | loop fusion | flops 16777216 | bytes 102760448 | tf_op jit(solution)/shard_map/add | solution.py:192
  1750.2 21.9 fusion.89
  1772.1 12.1 copy.125
  1784.3 10.6 copy.126
  1794.9 63.5 %fusion.30 = f32[2,8,8,256,128]{3,4,2,1,0:T(8,128)} fusion(f32[1,8,8,256,256]{4,3,0,2,1:T(8,128)} %bitcast.155, f32[1,8,8,256,256]{4,3,0,2,1:T(8,128)S(1)} %bitcast.154, f32[2,2,128,256,1,1]{2,3,1,0,5,4:T(8,128)S(1)} %copy-done.4), kind=kOutput, calls=%fused_computation.57 | convolution fusion | flops 25778192384 | bytes 50855936 | tf_op jit(solution)/shard_map/rbzyx,rokx->obzyk/dot_general | solution.py:30
  1858.4 10.1 slice_multiply_fusion.3
  1868.4 30.5 fusion.38
  1903.2 5.3 copy.87
  1908.5 5.3 copy.88
  1913.9 9.9 pad_maximum_fusion.2
  1923.8 79.3 %copy.89 = f32[2,8,8,16384]{2,1,0,3:T(8,128)} copy(f32[2,8,8,16384]{3,0,2,1:T(2,128)} %pad_maximum_fusion.2) | data formatting | bytes 16777216 | tf_op jit(solution)/shard_map/stack | solution.py:80
  2003.1 75.8 %reshape.320 = f32[32,1,65536]{2,1,0:T(1,128)} reshape(f32[16384,2,8,8]{3,2,1,0:T(8,128)} %bitcast.130) | data formatting | bytes 16777216
  2079.0 831.4 %all-to-all-start.1 = ((f32[32,1,65536]{2,1,0:T(1,128)}), f32[32,1,65536]{2,1,0:T(1,128)}, u32[]{:S(2)}, u32[]{:S(2)}) async-start(f32[32,1,65536]{2,1,0:T(1,128)} %reshape.320), calls=%async_computation.1 | async-start | bytes 16777216 | tf_op jit(solution)/shard_map/all_to_all | solution.py:194
  2910.4 5.4 copy.92
  2915.9 180.6 %all-to-all-done.1 = f32[32,1,65536]{2,1,0:T(1,128)} async-done(((f32[32,1,65536]{2,1,0:T(1,128)}), f32[32,1,65536]{2,1,0:T(1,128)}, u32[]{:S(2)}, u32[]{:S(2)}) %all-to-all-start.1) | async-done | bytes 8388640 | tf_op jit(solution)/shard_map/all_to_all | solution.py:194
  3097.0 25.1 reduce
  3122.1 123.4 %reshape.321 = f32[16384,2,8,8]{3,2,1,0:T(8,128)} reshape(f32[32,65536]{1,0:T(8,128)} %reduce) | data formatting | bytes 16777216
  3245.5 74.9 %copy.90 = f32[2,8,8,32,512]{4,2,3,1,0:T(8,128)} copy(f32[2,8,8,32,512]{2,1,0,4,3:T(8,128)} %bitcast.46) | data formatting | bytes 16777216 | tf_op jit(solution)/shard_map/all_to_all | solution.py:194
  3324.9 7.7 fusion.41
  3336.3 5.3 copy.93
  (143 shorter events, 83.1 us)
Async XLA Ops:
  0.6 31.5 copy-start
  23.9 8.5 copy-start.9
  23.9 193.7 %all-to-all-start = ((f32[2,8,256,512]{3,1,0,2:T(8,128)}), f32[2,8,256,512]{3,1,0,2:T(8,128)}, u32[]{:S(2)}, u32[]{:S(2)}) async-start(f32[2,8,256,512]{3,1,0,2:T(8,128)} %copy.78), calls=%async_computation | async-start | bytes 16777216 | tf_op jit(solution)/shard_map/all_to_all | solution.py:116
  395.0 257.7 %copy-start.7 = (f32[1,2,128,256]{2,3,1,0:T(8,128)S(1)}, f32[1,2,128,256]{2,3,1,0:T(8,128)}, u32[]{:S(2)}) copy-start(f32[1,2,128,256]{2,3,1,0:T(8,128)} %get-tuple-element.147) | copy-start | bytes 786436
  395.0 257.7 %copy-start.8 = (f32[1,2,128,256]{2,3,1,0:T(8,128)S(1)}, f32[1,2,128,256]{2,3,1,0:T(8,128)}, u32[]{:S(2)}) copy-start(f32[1,2,128,256]{2,3,1,0:T(8,128)} %get-tuple-element.152) | copy-start | bytes 786436
  395.1 258.8 %copy-start.6 = (f32[8,256,256]{2,1,0:T(8,128)S(1)}, f32[8,256,256]{2,1,0:T(8,128)}, u32[]{:S(2)}) copy-start(f32[8,256,256]{2,1,0:T(8,128)} %param.13) | copy-start | bytes 6291460
  519.7 125.9 %collective-permute-start = (f32[16,128]{1,0:T(8,128)S(1)}, f32[16,128]{1,0:T(8,128)S(1)}, u32[]{:S(2)}, u32[]{:S(2)}) collective-permute-start(f32[16,128]{1,0:T(8,128)S(1)} %get-tuple-element.153), channel_id=1, source_target_pairs={{2,0},{3,1},{4,2},{5,3},{6,4},{7,5},{8,6},{9,7},{10,8},{11,9},{12,... | collective-permute-start | bytes 24584 | tf_op jit(solution)/shard_map/ppermute | solution.py:17
  521.0 125.2 %collective-permute-start.1 = (f32[16,128]{1,0:T(8,128)S(1)}, f32[16,128]{1,0:T(8,128)S(1)}, u32[]{:S(2)}, u32[]{:S(2)}) collective-permute-start(f32[16,128]{1,0:T(8,128)S(1)} %get-tuple-element.156), channel_id=1, source_target_pairs={{1,0},{2,1},{3,2},{4,3},{5,4},{6,5},{7,6},{8,7},{9,8},{10,9},{11,1... | collective-permute-start | bytes 24584 | tf_op jit(solution)/shard_map/ppermute | solution.py:17
  644.8 6.7 collective-permute-start.2
  644.8 7.3 collective-permute-start.3
  652.7 10.9 collective-permute-start.4
  656.2 7.4 collective-permute-start.5
  656.2 7.4 collective-permute-start.6
  661.6 3.7 collective-permute-start.7
  1577.7 139.1 %copy-start.3 = (f32[256,2,8,128]{3,1,2,0:T(2,128)S(1)}, f32[256,2,8,128]{3,1,2,0:T(2,128)}, u32[]{:S(2)}) copy-start(f32[256,2,8,128]{3,1,2,0:T(2,128)} %copy.124) | copy-start | bytes 6291460
  1772.1 12.1 slice-start
  1772.1 12.1 slice-start.1
  1772.1 12.1 slice-start.2
  1772.1 12.1 slice-start.3
  1784.3 10.6 copy-start.4
  2079.0 1017.5 %all-to-all-start.1 = ((f32[32,1,65536]{2,1,0:T(1,128)}), f32[32,1,65536]{2,1,0:T(1,128)}, u32[]{:S(2)}, u32[]{:S(2)}) async-start(f32[32,1,65536]{2,1,0:T(1,128)} %reshape.320), calls=%async_computation.1 | async-start | bytes 16777216 | tf_op jit(solution)/shard_map/all_to_all | solution.py:194
  3320.4 4.5 copy-start.5
  3324.9 8.3 copy-start.2
  3333.2 8.4 copy-start.1
where the time goes:
time: 3370 us; the launch traced here: 3340 us
  starting transfers between devices  971 us (29%)
  other arithmetic  960 us (28%)
  local copies, waits for them, and re-layouts  854 us (25%)
  waiting for transfers between devices  374 us (11%)
  matrix products  180 us (5%)
    all_to_all x1, starting transfers between devices, per_device(): lax.all_to_all(grid_to_planes(applied[0], applied[1], cosine_lookup, sine...  831 us
    scatter-add x12, other arithmetic, apply_group(): return projected.at[:, offsets].add(slot_terms)  814 us
    unnamed x40, local copies, waits for them, and re-layouts  235 us
    all_to_all x1, waiting for transfers between devices, per_device(): lax.all_to_all(columns_to_planes(coefficients, cosine_lookup, sine_lookup...  185 us
    all_to_all x1, waiting for transfers between devices, per_device(): lax.all_to_all(grid_to_planes(applied[0], applied[1], cosine_lookup, sine...  181 us
    dot_general x6, matrix products, complex_step(): jnp.einsum(full_pattern, stacked, table, precision=lax.Precision.HIGHEST)  164 us
    while x1, local copies, waits for them, and re-layouts, per_device(): lax.fori_loop(0, groups_live, apply_group, jnp.zeros_like(fields))  139 us
    ppermute x8, starting transfers between devices, passed_along(): return lax.ppermute(block, axis, route)  132 us
  transfers between devices with their start and end apart: 10, of which 6 were waited for; matrix products, arithmetic and copies ran while one was open for 0% of the time, Pallas kernels for 0%

commit v1 on v0

--- a/solution.py
+++ b/solution.py
@@ -2,7 +2,11 @@
 
 import jax
 import jax.numpy as jnp
+import ml_dtypes
+import numpy as np
 from jax import lax
+from jax.experimental import pallas as pl
+from jax.experimental.pallas import tpu as pltpu
 from jax.sharding import PartitionSpec as P
 
 GRID_SIDE = 256
@@ -209,6 +213,350 @@
     return (applied_coefficients, becp_home)
 
 
+MIB = 1024 * 1024
+BF = jnp.bfloat16
+
+
+def split_table(table, axis):
+    high = table.astype(ml_dtypes.bfloat16)
+    low = (table - high.astype(np.float64)).astype(ml_dtypes.bfloat16)
+    return jnp.asarray(np.concatenate([high, high, low], axis))
+
+
+def split_data(data, axis):
+    high = data.astype(BF)
+    low = (data - high.astype(jnp.float32)).astype(BF)
+    return jnp.concatenate([high, low, high], axis)
+
+
+def host_tables(devices):
+    frequency = np.arange(WAVE_CUTOFF) - WAVE_CUTOFF // 2
+    turns = (np.arange(GRID_SIDE)[:, None] * frequency[None, :]) % GRID_SIDE
+    angle = 2.0 * np.pi / GRID_SIDE * turns
+    cosine, sine = np.cos(angle), np.sin(angle)
+    fwd = np.block([[cosine, -sine], [sine, cosine]]) * WAVE_CUTOFF ** (-0.5)
+    bwd = np.block([[cosine.T, sine.T], [-sine.T, cosine.T]]) * GRID_SIDE ** (-0.5)
+    width = WAVE_CUTOFF // devices
+    order = np.arange(WAVE_CUTOFF).reshape(devices, width).T.reshape(-1)
+    order = np.concatenate([order, WAVE_CUTOFF + order])
+    return fwd, bwd, fwd[:, order], bwd[order, :]
+
+
+def mm(left, right):
+    return jnp.dot(left, right, preferred_element_type=jnp.float32)
+
+
+def z_forward(coefficients, table, devices, width, zl):
+    bands = coefficients.shape[1]
+
+    def body(x_ref, t_ref, o_ref):
+        x = jnp.concatenate([x_ref[0, 0], x_ref[1, 0]], 1)
+        out = lax.dot_general(
+            t_ref[...], split_data(x, 1), (((1,), (1,)), ((), ())),
+            preferred_element_type=jnp.float32,
+        )
+        for c in range(2):
+            for k in range(width):
+                piece = out[c * GRID_SIDE:(c + 1) * GRID_SIDE, k * 128:(k + 1) * 128]
+                o_ref[:, 0, c, k] = piece.reshape(devices, zl, 128)
+
+    return pl.pallas_call(
+        body,
+        grid=(bands,),
+        in_specs=[
+            pl.BlockSpec((2, 1, width * 128, 128), lambda b: (0, b, 0, 0)),
+            pl.BlockSpec(table.shape, lambda b: (0, 0)),
+        ],
+        out_specs=pl.BlockSpec((devices, 1, 2, width, zl, 128), lambda b: (0, b, 0, 0, 0, 0)),
+        out_shape=jax.ShapeDtypeStruct((devices, bands, 2, width, zl, 128), jnp.float32),
+        compiler_params=pltpu.CompilerParams(vmem_limit_bytes=40 * MIB),
+        name="z_forward",
+    )(coefficients, table)
+
+
+def grid_and_gather(pieces, x_table, y_table, points, used, devices, width, zl, slots, npts):
+    bands = pieces.shape[1]
+    rows = 2 * width * zl
+    pieces = pieces.reshape(devices, bands, rows, 128)
+    total = zl * 4 * GRID_SIDE * 8
+
+    def body(points_ref, used_ref, r_ref, x_ref, y_ref, u_ref, g_ref):
+        band = pl.program_id(0)
+        flat = r_ref.reshape(devices * rows, 128)
+
+        @pl.loop(0, zl // 2)
+        def _(pair):
+            sides = []
+            for half in range(2):
+                z = pair * 2 + half
+                sides.append(jnp.concatenate(
+                    [flat[pl.ds(j * zl + z, devices, stride=rows), :] for j in range(2 * width)], 0
+                ))
+            first = mm(x_ref[...], split_data(jnp.concatenate(sides, 1), 0))
+            for half in range(2):
+                z = pair * 2 + half
+                lanes = slice(half * 128, half * 128 + 128)
+                left = jnp.concatenate([first[:GRID_SIDE, lanes], first[GRID_SIDE:, lanes]], 1)
+                second = mm(split_data(left, 1), y_ref[...])
+                for c in range(2):
+                    for yh in range(2):
+                        base = ((z * 2 + yh) * 2 + c) * GRID_SIDE * 8 + band
+                        u_ref[pl.ds(base, GRID_SIDE, stride=8), :] = second[
+                            :, c * 256 + yh * 128:c * 256 + yh * 128 + 128
+                        ]
+
+        @pl.when(band == bands - 1)
+        def _():
+            lane = lax.broadcasted_iota(jnp.int32, (8, 128), 1)
+
+            @pl.loop(0, used_ref[0])
+            def _(slot):
+                for part in range(npts // 128):
+                    first_point = slot * npts + part * 128
+
+                    def step(i, carry):
+                        real, imag = carry
+                        for q in range(16):
+                            t = i * 16 + q
+                            p = points_ref[first_point + t]
+                            row = pl.multiple_of((p >> 7) * 8, 8)
+                            shift = (t - p) & 127
+                            here = lane == t
+                            a = pltpu.roll(u_ref[pl.ds(row, 8), :], shift, 1)
+                            b = pltpu.roll(u_ref[pl.ds(row + GRID_SIDE * 8, 8), :], shift, 1)
+                            real = jnp.where(here, a, real)
+                            imag = jnp.where(here, b, imag)
+                        return real, imag
+
+                    zero = jnp.zeros((8, 128), jnp.float32)
+                    real, imag = lax.fori_loop(0, 8, step, (zero, zero))
+                    g_ref[slot, 0:8, part * 128:(part + 1) * 128] = real
+                    g_ref[slot, 8:16, part * 128:(part + 1) * 128] = imag
+
+    return pl.pallas_call(
+        body,
+        grid=(bands,),
+        in_specs=[
+            pl.BlockSpec(memory_space=pltpu.SMEM),
+            pl.BlockSpec(memory_space=pltpu.SMEM),
+            pl.BlockSpec((devices, 1, rows, 128), lambda b: (0, b, 0, 0)),
+            pl.BlockSpec(x_table.shape, lambda b: (0, 0)),
+            pl.BlockSpec(y_table.shape, lambda b: (0, 0)),
+        ],
+        out_specs=[
+            pl.BlockSpec((total, 128), lambda b: (0, 0), pipeline_mode=pl.Buffered(1)),
+            pl.BlockSpec((slots, 16, npts), lambda b: (0, 0, 0)),
+        ],
+        out_shape=[
+            jax.ShapeDtypeStruct((total, 128), jnp.float32),
+            jax.ShapeDtypeStruct((slots, 16, npts), jnp.float32),
+        ],
+        compiler_params=pltpu.CompilerParams(vmem_limit_bytes=58 * MIB),
+        name="grid_and_gather",
+    )(points, used, pieces, x_table, y_table)
+
+
+def scatter_and_back(field, pot, terms, y_table, x_table, points, used, devices, width, zl):
+    slots, _, npts = terms.shape
+    bands = 8
+    per_z = 4 * GRID_SIDE * 8
+    rows = 2 * width * bands
+
+    def body(points_ref, used_ref, u_ref, pot_ref, terms_ref, y_ref, x_ref, o_ref, acc_ref):
+        z = pl.program_id(0)
+
+        @pl.when(z == 0)
+        def _():
+            lane = lax.broadcasted_iota(jnp.int32, (8, 128), 1)
+
+            @pl.loop(0, zl * per_z // 512)
+            def _(i):
+                acc_ref[pl.ds(pl.multiple_of(i * 512, 512), 512), :] = jnp.zeros((512, 128), jnp.float32)
+
+            @pl.loop(0, used_ref[0])
+            def _(slot):
+                for part in range(npts // 128):
+                    first_point = slot * npts + part * 128
+                    real = terms_ref[slot, 0:8, part * 128:(part + 1) * 128]
+                    imag = terms_ref[slot, 8:16, part * 128:(part + 1) * 128]
+
+                    @pl.loop(0, 8)
+                    def _(i):
+                        for q in range(16):
+                            t = i * 16 + q
+                            p = points_ref[first_point + t]
+                            row = pl.multiple_of((p >> 7) * 8, 8)
+                            shift = (p - t) & 127
+                            here = lane == (p & 127)
+                            a = jnp.where(here, pltpu.roll(real, shift, 1), 0.0)
+                            b = jnp.where(here, pltpu.roll(imag, shift, 1), 0.0)
+                            acc_ref[pl.ds(row, 8), :] += a
+                            acc_ref[pl.ds(row + GRID_SIDE * 8, 8), :] += b
+
+        flat = o_ref.reshape(devices * rows, 128)
+
+        @pl.loop(0, bands // 2)
+        def _(pair):
+            sides = []
+            for half in range(2):
+                band = pair * 2 + half
+                cols = []
+                for c in range(2):
+                    for yh in range(2):
+                        base = (yh * 2 + c) * GRID_SIDE * 8 + band
+                        cols.append(
+                            u_ref[pl.ds(base, GRID_SIDE, stride=8), :] * pot_ref[0, yh]
+                            + acc_ref[pl.ds(z * per_z + base, GRID_SIDE, stride=8), :]
+                        )
+                first = mm(split_data(jnp.concatenate(cols, 1), 1), y_ref[...])
+                sides.append(jnp.concatenate([first[:, :128], first[:, 128:]], 0))
+            second = mm(x_ref[...], split_data(jnp.concatenate(sides, 1), 0))
+            for half in range(2):
+                band = pair * 2 + half
+                for j in range(2 * width):
+                    flat[pl.ds(j * bands + band, devices, stride=rows), :] = second[
+                        j * devices:(j + 1) * devices, half * 128:half * 128 + 128
+                    ]
+
+    return pl.pallas_call(
+        body,
+        grid=(zl,),
+        in_specs=[
+            pl.BlockSpec(memory_space=pltpu.SMEM),
+            pl.BlockSpec(memory_space=pltpu.SMEM),
+            pl.BlockSpec((per_z, 128), lambda z: (z, 0)),
+            pl.BlockSpec((1, 2, GRID_SIDE, 128), lambda z: (z, 0, 0, 0)),
+            pl.BlockSpec(terms.shape, lambda z: (0, 0, 0)),
+            pl.BlockSpec(y_table.shape, lambda z: (0, 0)),
+            pl.BlockSpec(x_table.shape, lambda z: (0, 0)),
+        ],
+        out_specs=pl.BlockSpec((devices, 1, rows, 128), lambda z: (0, z, 0, 0)),
+        out_shape=jax.ShapeDtypeStruct((devices, zl, rows, 128), jnp.float32),
+        scratch_shapes=[pltpu.VMEM((zl * per_z, 128), jnp.float32)],
+        compiler_params=pltpu.CompilerParams(vmem_limit_bytes=60 * MIB),
+        name="scatter_and_back",
+    )(points, used, field, pot, terms, y_table, x_table)
+
+
+def z_backward(pieces, table, coefficients, device, devices, width, zl):
+    bands = 8
+    rows = 2 * width * bands
+    pieces = pieces.reshape(devices * zl * rows, 128)
+
+    def body(dev_ref, r_ref, t_ref, c_ref, o_ref):
+        band = pl.program_id(0)
+        fy = lax.broadcasted_iota(jnp.int32, (128, 128), 0) - WAVE_CUTOFF // 2
+        fz = lax.broadcasted_iota(jnp.int32, (128, 128), 1) - WAVE_CUTOFF // 2
+        for k in range(width):
+            data = jnp.concatenate(
+                [r_ref[pl.ds((c * width + k) * bands + band, GRID_SIDE, stride=rows), :] for c in range(2)], 0
+            )
+            res = mm(split_data(data.T, 1), t_ref[...])
+            fx = dev_ref[0] * width + k - WAVE_CUTOFF // 2
+            kinetic = 6.0 / (WAVE_CUTOFF * WAVE_CUTOFF) * (fy * fy + fz * fz + fx * fx).astype(jnp.float32)
+            for c in range(2):
+                o_ref[c, 0, k * 128:(k + 1) * 128, :] = (
+                    res[:, c * 128:(c + 1) * 128] + kinetic * c_ref[c, 0, k * 128:(k + 1) * 128, :]
+                )
+
+    spec = pl.BlockSpec((2, 1, width * 128, 128), lambda b: (0, b, 0, 0))
+    return pl.pallas_call(
+        body,
+        grid=(bands,),
+        in_specs=[
+            pl.BlockSpec(memory_space=pltpu.SMEM),
+            pl.BlockSpec(pieces.shape, lambda b: (0, 0), pipeline_mode=pl.Buffered(1)),
+            pl.BlockSpec(table.shape, lambda b: (0, 0)),
+            spec,
+        ],
+        out_specs=spec,
+        out_shape=jax.ShapeDtypeStruct(coefficients.shape, jnp.float32),
+        compiler_params=pltpu.CompilerParams(vmem_limit_bytes=48 * MIB),
+        name="z_backward",
+    )(device.reshape(1), pieces, table, coefficients)
+
+
+def per_device_fast(
+    coefficients,
+    potential,
+    slot_atom,
+    slot_count,
+    point_offset,
+    proj_value,
+    proj_strength,
+    proj_count,
+):
+    highest = lax.Precision.HIGHEST
+    device = lax.axis_index("pencil")
+    devices = lax.axis_size("pencil")
+    width = coefficients.shape[2] // WAVE_CUTOFF
+    zl = potential.shape[0]
+    slots, npts = point_offset.shape
+    fwd, bwd, fwd_x, bwd_x = host_tables(devices)
+    sent = z_forward(coefficients, split_table(fwd, 1), devices, width, zl)
+    pieces = lax.all_to_all(sent, "pencil", split_axis=0, concat_axis=0, tiled=True)
+    z = point_offset // (GRID_SIDE * GRID_SIDE)
+    y = point_offset // GRID_SIDE % GRID_SIDE
+    x = point_offset % GRID_SIDE
+    points = (((z * 2 + y // 128) * 2 * GRID_SIDE + x) * 128 + y % 128).reshape(-1)
+    used = slot_count
+    field, picked = grid_and_gather(
+        pieces, split_table(fwd_x, 1), split_table(fwd.T, 0), points, used,
+        devices, width, zl, slots, npts,
+    )
+    live = jnp.arange(slots, dtype=jnp.int32) < used[0]
+    coeffs = jnp.einsum("smt,spt->smp", picked, proj_value, precision=highest)
+    coeff_width = 16 * NPROJ
+    coeffs = jnp.where(live[:, None, None], coeffs, 0.0).reshape(slots, coeff_width)
+    atom_dev = proj_strength.shape[0] // devices
+    column_proj = jnp.arange(coeff_width, dtype=jnp.int32) % NPROJ
+    window_size = 2 * REACH + 1
+    relative = (slot_atom // atom_dev - device + REACH) % devices
+    window_index = relative * atom_dev + slot_atom % atom_dev
+    onehot = (
+        window_index[:, None] == jnp.arange(window_size * atom_dev, dtype=jnp.int32)[None, :]
+    ).astype(jnp.float32)
+    partial_sum = jnp.dot(onehot.T, coeffs, precision=highest).reshape(
+        window_size, atom_dev, coeff_width
+    )
+    count_home = lax.dynamic_slice_in_dim(proj_count, device * atom_dev, atom_dev, 0)
+    mask_home = column_proj[None, :] < count_home[:, None]
+    strength_home = jnp.tile(
+        lax.dynamic_slice_in_dim(proj_strength, device * atom_dev, atom_dev, 0), (1, 16)
+    )
+    totals = partial_sum[REACH]
+    for offset in range(-REACH, REACH + 1):
+        if offset != 0:
+            totals = totals + passed_along(partial_sum[REACH + offset], "pencil", offset)
+    becp_home = jnp.where(mask_home, totals, 0.0)
+    energy_home = becp_home * strength_home
+    window = jnp.concatenate(
+        [
+            energy_home if offset == 0 else passed_along(energy_home, "pencil", -offset)
+            for offset in range(-REACH, REACH + 1)
+        ],
+        0,
+    )
+    energy = jnp.dot(onehot, window, precision=highest).reshape(slots, 16, NPROJ)
+    terms = jnp.einsum("smp,spt->smt", energy, proj_value, precision=highest)
+    pot = potential.reshape(zl, 2, 128, GRID_SIDE).transpose(0, 1, 3, 2)
+    back = scatter_and_back(
+        field, pot, terms, split_table(bwd.T, 0), split_table(bwd_x, 1), points, used,
+        devices, width, zl,
+    )
+    pieces = lax.all_to_all(back, "pencil", split_axis=0, concat_axis=0, tiled=True)
+    applied_coefficients = z_backward(
+        pieces, split_table(bwd.T, 0), coefficients, device, devices, width, zl
+    )
+    return (applied_coefficients, becp_home)
+
+
+def per_device_any(coefficients, potential, *rest):
+    whole_tiles = potential.shape[0] % 8 == 0 and coefficients.shape[1] == 8
+    body = per_device_fast if whole_tiles else per_device
+    return body(coefficients, potential, *rest)
+
+
 def solution(mesh):
     in_specs = (
         P(None, None, "pencil", None),
@@ -222,5 +570,5 @@
     )
     out_specs = (P(None, None, "pencil", None), P("pencil", None))
     return jax.shard_map(
-        per_device, mesh=mesh, in_specs=in_specs, out_specs=out_specs, check_vma=False
-    )
+        per_device_any, mesh=mesh, in_specs=in_specs, out_specs=out_specs, check_vma=False
+    )

time: 3370 us -> 789 us (0.23)
  other arithmetic: 960 us -> 0.88 us
  starting transfers between devices: 971 us -> 17.4 us
  local copies, waits for them, and re-layouts: 854 us -> 11 us
  blocking collectives: 0 us -> 303 us
  Pallas kernels: 0 us -> 258 us
  waiting for transfers between devices: 374 us -> 190 us
  matrix products: 180 us -> 4.86 us
    all_to_all x2 -> x1, starting transfers between devices: 839 us -> 7.43 us  [per_device_fast(): lax.all_to_all(sent, 'pencil', split_axis=0, concat_axis=0, tiled=True)]
    scatter-add x12 -> x0, other arithmetic: 814 us -> none  [apply_group(): return projected.at[:, offsets].add(slot_terms)]
    all_to_all x0 -> x1, blocking collectives: none -> 303 us  [per_device_fast(): lax.all_to_all(back, 'pencil', split_axis=0, concat_axis=0, tiled=True)]
    pallas_call x0 -> x4, Pallas kernels: none -> 258 us  [the longest x1 127 us: scatter_and_back(): pl.pallas_call(body, grid=(zl,), in_specs=[pl.BlockSpec(memory_space=pltp...]
    unnamed x40 -> x25, local copies, waits for them, and re-layouts: 235 us -> 7.33 us
    all_to_all x2 -> x1, waiting for transfers between devices: 366 us -> 184 us  [per_device_fast(): lax.all_to_all(sent, 'pencil', split_axis=0, concat_axis=0, tiled=True)]
    dot_general x12 -> x4, matrix products: 169 us -> 4.86 us  [the longest x1 2.23 us: per_device_fast(): coeffs = jnp.einsum('smt,spt->smp', picked, proj_value, precision=highest)]
    while x9 -> x0, local copies, waits for them, and re-layouts: 139 us -> none  [the longest x1 139 us: per_device(): lax.fori_loop(0, groups_live, apply_group, jnp.zeros_like(fields))]
  transfers between devices with their start and end apart: 10 -> 9, of which waited for: 6 -> 5; matrix products, arithmetic and copies ran while one was open for 0% -> 1% of each run, Pallas kernels for 0% -> 0%
where the time goes in v1:
time: 789 us; the launch traced here: 787 us
  blocking collectives  303 us (38%)
  Pallas kernels  258 us (33%)
  waiting for transfers between devices  190 us (24%)
  starting transfers between devices  17.4 us (2%)
  local copies, waits for them, and re-layouts  11 us (1%)
    all_to_all x1, blocking collectives, per_device_fast(): lax.all_to_all(back, 'pencil', split_axis=0, concat_axis=0, tiled=True)  303 us
    all_to_all x1, waiting for transfers between devices, per_device_fast(): lax.all_to_all(sent, 'pencil', split_axis=0, concat_axis=0, tiled=True)  184 us
    pallas_call x1, Pallas kernels, scatter_and_back(): pl.pallas_call(body, grid=(zl,), in_specs=[pl.BlockSpec(memory_space=pltp...  127 us
    pallas_call x1, Pallas kernels, grid_and_gather(): pl.pallas_call(body, grid=(bands,), in_specs=[pl.BlockSpec(memory_space=p...  112 us
  transfers between devices with their start and end apart: 9, of which 5 were waited for; matrix products, arithmetic and copies ran while one was open for 1% of the time, Pallas kernels for 0%

profile of v1, /device:TPU:0, one launch (start us, length us, event | category | flops | bytes accessed | tf_op | source)
XLA Modules:
  0.0 787.0 jit_solution(14964474304721265769)
XLA Ops:
  0.6 0.0 copy-start
  0.6 0.0 copy-start.3
  0.7 2.2 copy-done.3
  2.9 1.1 copy-done.6
  4.0 5.7 z_forward.1
  9.7 0.0 copy-start.2
  9.7 3.2 copy-done.2
  13.0 7.4 all-to-all-start
  20.4 0.0 copy-start.7
  21.2 0.0 copy-done.8
  21.2 0.2 fusion.7
  21.4 0.7 copy.24
  22.1 0.8 constant_dynamic-slice_fusion
  22.9 0.0 copy-done.9
  22.9 183.6 %all-to-all-done = f32[32,8,2,4,8,128]{5,4,3,2,1,0:T(8,128)} async-done(((f32[32,8,2,4,8,128]{5,4,3,2,1,0:T(8,128)}), f32[32,8,2,4,8,128]{5,4,3,2,1,0:T(8,128)}, u32[]{:S(2)}, u32[]{:S(2)}) %all-to-all-start) | async-done | bytes 8388640 | tf_op jit(solution)/shard_map/all_to_all | solution.py:497
  206.5 111.6 %grid_and_gather.1 = (f32[65536,128]{1,0:T(8,128)}, f32[64,16,256]{2,1,0:T(8,128)}) custom-call(s32[16384]{0:T(1024)} %bitcast.25, s32[1]{0:T(128)} %copy.29.used_ref, f32[32,8,64,128]{3,2,1,0:T(8,128)} %bitcast.1.r_ref, bf16[512,768]{1,0:T(8,128)(2,1)} %constant.139.clone.x_ref, bf16[768,512]{1,0:T(8,128)(2,1)} %constant.140.clone.y_ref), custom_call_target="tpu_custom_call" | custom-call | tf_op jit(solution)/shard_map/grid_and_gather/pallas_call | solution.py:336
  318.1 0.0 copy-done
  318.1 2.2 convolution_select_fusion
  320.3 0.1 copy.19
  320.4 0.3 fusion.9
  320.8 0.1 collective-permute-start
  320.8 0.1 collective-permute-start.1
  320.9 0.5 collective-permute-start.2
  321.4 2.0 collective-permute-start.3
  323.4 0.8 dynamic_slice.6
  324.2 0.3 collective-permute-done
  324.5 0.0 collective-permute-done.1
  324.5 3.1 collective-permute-done.2
  327.6 1.0 collective-permute-done.3
  328.6 0.7 fusion.28
  329.3 0.0 collective-permute-start.4
  329.3 0.0 copy-done.7
  329.3 1.8 copy.18
  331.1 0.4 collective-permute-start.5
  331.5 5.0 collective-permute-start.6
  336.5 2.0 collective-permute-start.7
  338.5 0.0 collective-permute-done.4
  338.5 0.0 collective-permute-done.5
  338.5 0.0 collective-permute-done.6
  338.5 1.6 collective-permute-done.7
  340.2 0.3 convolution_bitcast_fusion
  340.4 0.2 copy.22
  340.6 2.0 fusion.31.terms_ref
  342.6 127.5 %scatter_and_back.1 = f32[32,8,64,128]{3,2,1,0:T(8,128)} custom-call(s32[16384]{0:T(1024)} %bitcast.26, s32[1]{0:T(128)} %copy.29.used_ref, f32[65536,128]{1,0:T(8,128)} %get-tuple-element.4.u_ref, f32[8,2,256,128]{3,2,1,0:T(8,128)} %bitcast.23, f32[64,16,256]{2,1,0:T(8,128)} %fusion.31.terms_ref, bf16[1536,256]{1,0:T(8,128)(2,1)} %constant.141.clone.y_ref.t_ref, ...), custom_call_target="tpu_custom_call" | custom-call | tf_op jit(solution)/shard_map/scatter_and_back/pallas_call | solution.py:421
  470.1 303.2 %all_to_all.10 = f32[32,8,64,128]{3,2,1,0:T(8,128)} all-to-all(f32[32,8,64,128]{3,2,1,0:T(8,128)} %scatter_and_back.1), channel_id=1, replica_groups=mesh['pencil'=32] {'pencil'}, dimensions={0} | all-to-all | bytes 16777216 | tf_op jit(solution)/shard_map/all_to_all | solution.py:547
  773.3 0.0 copy-done.4
  773.3 0.0 copy-done.5
  773.3 13.7 %z_backward.1 = f32[2,8,512,128]{3,2,1,0:T(8,128)} custom-call(s32[1]{0:T(128)} %bitcast.dev_ref, f32[16384,128]{1,0:T(8,128)} %bitcast.22, bf16[1536,256]{1,0:T(8,128)(2,1)S(1)} %copy-done.5, f32[2,8,512,128]{3,2,1,0:T(8,128)S(1)} %copy-done.4), custom_call_target="tpu_custom_call" | custom-call | tf_op jit(solution)/shard_map/z_backward/pallas_call | solution.py:463
  (18 shorter events, 0.1 us)
Async XLA Ops:
  0.6 317.4 %copy-start = (f32[64,8,256]{2,1,0:T(8,128)S(1)}, f32[64,8,256]{2,1,0:T(8,128)}, u32[]{:S(2)}) copy-start(f32[64,8,256]{2,1,0:T(8,128)} %param.19) | copy-start | bytes 1572868
  0.6 2.2 copy-start.3
  2.9 1.1 copy-start.6
  9.7 3.3 copy-start.2
  13.0 8.3 %copy-start.8 = (s32[64,256]{1,0:T(8,128)S(1)}, s32[64,256]{1,0:T(8,128)}, u32[]{:S(2)}) copy-start(s32[64,256]{1,0:T(8,128)} %param.18) | copy-start | bytes 196612
  13.0 9.9 %copy-start.9 = (s32[64]{0:T(128)S(1)}, s32[64]{0:T(128)}, u32[]{:S(2)}) copy-start(s32[64]{0:T(128)} %param.16) | copy-start | bytes 772
  13.0 193.5 %all-to-all-start = ((f32[32,8,2,4,8,128]{5,4,3,2,1,0:T(8,128)}), f32[32,8,2,4,8,128]{5,4,3,2,1,0:T(8,128)}, u32[]{:S(2)}, u32[]{:S(2)}) async-start(f32[32,8,2,4,8,128]{5,4,3,2,1,0:T(8,128)} %copy-done.2), calls=%async_computation | async-start | bytes 16777216 | tf_op jit(solution)/shard_map/all_to_all | solution.py:497
  20.4 308.9 %copy-start.7 = (f32[8,256,256]{2,1,0:T(8,128)S(1)}, f32[8,256,256]{2,1,0:T(8,128)}, u32[]{:S(2)}) copy-start(f32[8,256,256]{2,1,0:T(8,128)} %param.15) | copy-start | bytes 6291460
  320.8 3.7 collective-permute-start
  320.8 3.6 collective-permute-start.1
  320.9 6.7 collective-permute-start.2
  321.4 7.2 collective-permute-start.3
  329.3 9.2 %collective-permute-start.4 = (f32[16,128]{1,0:T(8,128)S(1)}, f32[16,128]{1,0:T(8,128)S(1)}, u32[]{:S(2)}, u32[]{:S(2)}) collective-permute-start(f32[16,128]{1,0:T(8,128)S(1)} %get-tuple-element.6), channel_id=1, source_target_pairs={{30,0},{31,1},{0,2},{1,3},{2,4},{3,5},{4,6},{5,7},{6,8},{7,9},{8,1... | collective-permute-start | bytes 24584 | tf_op jit(solution)/shard_map/ppermute | solution.py:21
  331.1 7.4 collective-permute-start.5
  331.5 7.0 collective-permute-start.6
  336.5 3.7 collective-permute-start.7
  470.1 303.2 %copy-start.4 = (f32[2,8,512,128]{3,2,1,0:T(8,128)S(1)}, f32[2,8,512,128]{3,2,1,0:T(8,128)}, u32[]{:S(2)}) copy-start(f32[2,8,512,128]{3,2,1,0:T(8,128)} %c_ref.1) | copy-start | bytes 12582916
  470.1 303.2 %copy-start.5 = (bf16[1536,256]{1,0:T(8,128)(2,1)S(1)}, bf16[1536,256]{1,0:T(8,128)(2,1)}, u32[]{:S(2)}) copy-start(bf16[1536,256]{1,0:T(8,128)(2,1)} %constant.141.clone.y_ref.t_ref) | copy-start | bytes 2359300
  773.3 13.7 %copy-start.1 = (f32[64,8,256]{2,1,0:T(8,128)S(1)}, f32[64,8,256]{2,1,0:T(8,128)}, u32[]{:S(2)}) copy-start(f32[64,8,256]{2,1,0:T(8,128)} %param.19) | copy-start | bytes 1572868

commit v2 on v1

--- a/solution.py
+++ b/solution.py
@@ -215,6 +215,11 @@
 
 MIB = 1024 * 1024
 BF = jnp.bfloat16
+HALF = 4
+
+
+def cost(flops, moved):
+    return pl.CostEstimate(flops=flops, bytes_accessed=moved, transcendentals=0)
 
 
 def split_table(table, axis):
@@ -246,8 +251,8 @@
     return jnp.dot(left, right, preferred_element_type=jnp.float32)
 
 
-def z_forward(coefficients, table, devices, width, zl):
-    bands = coefficients.shape[1]
+def z_forward(coefficients, table, part, devices, width, zl):
+    bands = HALF
 
     def body(x_ref, t_ref, o_ref):
         x = jnp.concatenate([x_ref[0, 0], x_ref[1, 0]], 1)
@@ -264,23 +269,24 @@
         body,
         grid=(bands,),
         in_specs=[
-            pl.BlockSpec((2, 1, width * 128, 128), lambda b: (0, b, 0, 0)),
+            pl.BlockSpec((2, 1, width * 128, 128), lambda b: (0, b + part * HALF, 0, 0)),
             pl.BlockSpec(table.shape, lambda b: (0, 0)),
         ],
         out_specs=pl.BlockSpec((devices, 1, 2, width, zl, 128), lambda b: (0, b, 0, 0, 0, 0)),
         out_shape=jax.ShapeDtypeStruct((devices, bands, 2, width, zl, 128), jnp.float32),
-        compiler_params=pltpu.CompilerParams(vmem_limit_bytes=40 * MIB),
+        compiler_params=pltpu.CompilerParams(vmem_limit_bytes=32 * MIB),
+        cost_estimate=cost(3 * 2**30, 8 * MIB),
         name="z_forward",
     )(coefficients, table)
 
 
-def grid_and_gather(pieces, x_table, y_table, points, used, devices, width, zl, slots, npts):
+def grid_and_gather(pieces, x_table, y_table, point_rows, shifts, used, devices, width, zl, slots, npts):
     bands = pieces.shape[1]
     rows = 2 * width * zl
     pieces = pieces.reshape(devices, bands, rows, 128)
-    total = zl * 4 * GRID_SIDE * 8
-
-    def body(points_ref, used_ref, r_ref, x_ref, y_ref, u_ref, g_ref):
+    total = zl * 2 * GRID_SIDE * 8
+
+    def body(rows_ref, shifts_ref, used_ref, r_ref, x_ref, y_ref, u_ref, g_ref):
         band = pl.program_id(0)
         flat = r_ref.reshape(devices * rows, 128)
 
@@ -300,7 +306,7 @@
                 second = mm(split_data(left, 1), y_ref[...])
                 for c in range(2):
                     for yh in range(2):
-                        base = ((z * 2 + yh) * 2 + c) * GRID_SIDE * 8 + band
+                        base = (z * 2 + yh) * GRID_SIDE * 8 + c * HALF + band
                         u_ref[pl.ds(base, GRID_SIDE, stride=8), :] = second[
                             :, c * 256 + yh * 128:c * 256 + yh * 128 + 128
                         ]
@@ -309,34 +315,21 @@
         def _():
             lane = lax.broadcasted_iota(jnp.int32, (8, 128), 1)
 
-            @pl.loop(0, used_ref[0])
-            def _(slot):
-                for part in range(npts // 128):
-                    first_point = slot * npts + part * 128
-
-                    def step(i, carry):
-                        real, imag = carry
-                        for q in range(16):
-                            t = i * 16 + q
-                            p = points_ref[first_point + t]
-                            row = pl.multiple_of((p >> 7) * 8, 8)
-                            shift = (t - p) & 127
-                            here = lane == t
-                            a = pltpu.roll(u_ref[pl.ds(row, 8), :], shift, 1)
-                            b = pltpu.roll(u_ref[pl.ds(row + GRID_SIDE * 8, 8), :], shift, 1)
-                            real = jnp.where(here, a, real)
-                            imag = jnp.where(here, b, imag)
-                        return real, imag
-
-                    zero = jnp.zeros((8, 128), jnp.float32)
-                    real, imag = lax.fori_loop(0, 8, step, (zero, zero))
-                    g_ref[slot, 0:8, part * 128:(part + 1) * 128] = real
-                    g_ref[slot, 8:16, part * 128:(part + 1) * 128] = imag
+            @pl.loop(0, used_ref[0] * (npts // 128))
+            def _(group):
+                first_point = group * 128
+                sums = [jnp.zeros((8, 128), jnp.float32) for _ in range(4)]
+                for t in range(128):
+                    row = pl.multiple_of(rows_ref[first_point + t], 8)
+                    tile = pltpu.roll(u_ref[pl.ds(row, 8), :], shifts_ref[first_point + t], 1)
+                    sums[t % 4] = jnp.where(lane == t, tile, sums[t % 4])
+                g_ref[group] = (sums[0] + sums[1]) + (sums[2] + sums[3])
 
     return pl.pallas_call(
         body,
         grid=(bands,),
         in_specs=[
+            pl.BlockSpec(memory_space=pltpu.SMEM),
             pl.BlockSpec(memory_space=pltpu.SMEM),
             pl.BlockSpec(memory_space=pltpu.SMEM),
             pl.BlockSpec((devices, 1, rows, 128), lambda b: (0, b, 0, 0)),
@@ -345,24 +338,25 @@
         ],
         out_specs=[
             pl.BlockSpec((total, 128), lambda b: (0, 0), pipeline_mode=pl.Buffered(1)),
-            pl.BlockSpec((slots, 16, npts), lambda b: (0, 0, 0)),
+            pl.BlockSpec((slots * npts // 128, 8, 128), lambda b: (0, 0, 0)),
         ],
         out_shape=[
             jax.ShapeDtypeStruct((total, 128), jnp.float32),
-            jax.ShapeDtypeStruct((slots, 16, npts), jnp.float32),
+            jax.ShapeDtypeStruct((slots * npts // 128, 8, 128), jnp.float32),
         ],
-        compiler_params=pltpu.CompilerParams(vmem_limit_bytes=58 * MIB),
+        compiler_params=pltpu.CompilerParams(vmem_limit_bytes=32 * MIB),
+        cost_estimate=cost(12 * 2**30, 192 * MIB),
         name="grid_and_gather",
-    )(points, used, pieces, x_table, y_table)
-
-
-def scatter_and_back(field, pot, terms, y_table, x_table, points, used, devices, width, zl):
+    )(point_rows, shifts, used, pieces, x_table, y_table)
+
+
+def scatter_and_back(field, pot, terms, y_table, x_table, point_rows, shifts, used, devices, width, zl):
     slots, _, npts = terms.shape
-    bands = 8
-    per_z = 4 * GRID_SIDE * 8
+    bands = HALF
+    per_z = 2 * GRID_SIDE * 8
     rows = 2 * width * bands
 
-    def body(points_ref, used_ref, u_ref, pot_ref, terms_ref, y_ref, x_ref, o_ref, acc_ref):
+    def body(rows_ref, shifts_ref, used_ref, u_ref, pot_ref, terms_ref, y_ref, x_ref, o_ref, acc_ref):
         z = pl.program_id(0)
 
         @pl.when(z == 0)
@@ -377,21 +371,11 @@
             def _(slot):
                 for part in range(npts // 128):
                     first_point = slot * npts + part * 128
-                    real = terms_ref[slot, 0:8, part * 128:(part + 1) * 128]
-                    imag = terms_ref[slot, 8:16, part * 128:(part + 1) * 128]
-
-                    @pl.loop(0, 8)
-                    def _(i):
-                        for q in range(16):
-                            t = i * 16 + q
-                            p = points_ref[first_point + t]
-                            row = pl.multiple_of((p >> 7) * 8, 8)
-                            shift = (p - t) & 127
-                            here = lane == (p & 127)
-                            a = jnp.where(here, pltpu.roll(real, shift, 1), 0.0)
-                            b = jnp.where(here, pltpu.roll(imag, shift, 1), 0.0)
-                            acc_ref[pl.ds(row, 8), :] += a
-                            acc_ref[pl.ds(row + GRID_SIDE * 8, 8), :] += b
+                    term = terms_ref[slot, :, part * 128:(part + 1) * 128]
+                    for t in range(128):
+                        row = pl.multiple_of(rows_ref[first_point + t], 8)
+                        alone = jnp.where(lane == t, term, 0.0)
+                        acc_ref[pl.ds(row, 8), :] += pltpu.roll(alone, shifts_ref[first_point + t], 1)
 
         flat = o_ref.reshape(devices * rows, 128)
 
@@ -403,7 +387,7 @@
                 cols = []
                 for c in range(2):
                     for yh in range(2):
-                        base = (yh * 2 + c) * GRID_SIDE * 8 + band
+                        base = yh * GRID_SIDE * 8 + c * HALF + band
                         cols.append(
                             u_ref[pl.ds(base, GRID_SIDE, stride=8), :] * pot_ref[0, yh]
                             + acc_ref[pl.ds(z * per_z + base, GRID_SIDE, stride=8), :]
@@ -414,7 +398,7 @@
             for half in range(2):
                 band = pair * 2 + half
                 for j in range(2 * width):
-                    flat[pl.ds(j * bands + band, devices, stride=rows), :] = second[
+                    flat[pl.ds((j % width * 2 + j // width) * bands + band, devices, stride=rows), :] = second[
                         j * devices:(j + 1) * devices, half * 128:half * 128 + 128
                     ]
 
@@ -422,6 +406,7 @@
         body,
         grid=(zl,),
         in_specs=[
+            pl.BlockSpec(memory_space=pltpu.SMEM),
             pl.BlockSpec(memory_space=pltpu.SMEM),
             pl.BlockSpec(memory_space=pltpu.SMEM),
             pl.BlockSpec((per_z, 128), lambda z: (z, 0)),
@@ -433,23 +418,25 @@
         out_specs=pl.BlockSpec((devices, 1, rows, 128), lambda z: (0, z, 0, 0)),
         out_shape=jax.ShapeDtypeStruct((devices, zl, rows, 128), jnp.float32),
         scratch_shapes=[pltpu.VMEM((zl * per_z, 128), jnp.float32)],
-        compiler_params=pltpu.CompilerParams(vmem_limit_bytes=60 * MIB),
+        compiler_params=pltpu.CompilerParams(vmem_limit_bytes=36 * MIB),
+        cost_estimate=cost(12 * 2**30, 256 * MIB),
         name="scatter_and_back",
-    )(points, used, field, pot, terms, y_table, x_table)
-
-
-def z_backward(pieces, table, coefficients, device, devices, width, zl):
-    bands = 8
+    )(point_rows, shifts, used, field, pot, terms, y_table, x_table)
+
+
+def z_backward(pieces, table, coefficients, before, part, device, devices, width, zl):
+    bands = HALF
     rows = 2 * width * bands
     pieces = pieces.reshape(devices * zl * rows, 128)
 
-    def body(dev_ref, r_ref, t_ref, c_ref, o_ref):
+    def body(dev_ref, r_ref, t_ref, c_ref, *rest):
+        o_ref = rest[-1]
         band = pl.program_id(0)
         fy = lax.broadcasted_iota(jnp.int32, (128, 128), 0) - WAVE_CUTOFF // 2
         fz = lax.broadcasted_iota(jnp.int32, (128, 128), 1) - WAVE_CUTOFF // 2
         for k in range(width):
             data = jnp.concatenate(
-                [r_ref[pl.ds((c * width + k) * bands + band, GRID_SIDE, stride=rows), :] for c in range(2)], 0
+                [r_ref[pl.ds((k * 2 + c) * bands + band, GRID_SIDE, stride=rows), :] for c in range(2)], 0
             )
             res = mm(split_data(data.T, 1), t_ref[...])
             fx = dev_ref[0] * width + k - WAVE_CUTOFF // 2
@@ -459,21 +446,30 @@
                     res[:, c * 128:(c + 1) * 128] + kinetic * c_ref[c, 0, k * 128:(k + 1) * 128, :]
                 )
 
-    spec = pl.BlockSpec((2, 1, width * 128, 128), lambda b: (0, b, 0, 0))
+    spec = pl.BlockSpec((2, 1, width * 128, 128), lambda b: (0, b + part * HALF, 0, 0))
+    in_specs = [
+        pl.BlockSpec(memory_space=pltpu.SMEM),
+        pl.BlockSpec(pieces.shape, lambda b: (0, 0), pipeline_mode=pl.Buffered(1)),
+        pl.BlockSpec(table.shape, lambda b: (0, 0)),
+        spec,
+    ]
+    operands = [device.reshape(1), pieces, table, coefficients]
+    aliases = {}
+    if before is not None:
+        in_specs.append(pl.BlockSpec(memory_space=pl.ANY))
+        operands.append(before)
+        aliases = {4: 0}
     return pl.pallas_call(
         body,
         grid=(bands,),
-        in_specs=[
-            pl.BlockSpec(memory_space=pltpu.SMEM),
-            pl.BlockSpec(pieces.shape, lambda b: (0, 0), pipeline_mode=pl.Buffered(1)),
-            pl.BlockSpec(table.shape, lambda b: (0, 0)),
-            spec,
-        ],
+        in_specs=in_specs,
         out_specs=spec,
         out_shape=jax.ShapeDtypeStruct(coefficients.shape, jnp.float32),
-        compiler_params=pltpu.CompilerParams(vmem_limit_bytes=48 * MIB),
+        input_output_aliases=aliases,
+        compiler_params=pltpu.CompilerParams(vmem_limit_bytes=32 * MIB),
+        cost_estimate=cost(3 * 2**30, 24 * MIB),
         name="z_backward",
-    )(device.reshape(1), pieces, table, coefficients)
+    )(*operands)
 
 
 def per_device_fast(
@@ -493,21 +489,35 @@
     zl = potential.shape[0]
     slots, npts = point_offset.shape
     fwd, bwd, fwd_x, bwd_x = host_tables(devices)
-    sent = z_forward(coefficients, split_table(fwd, 1), devices, width, zl)
-    pieces = lax.all_to_all(sent, "pencil", split_axis=0, concat_axis=0, tiled=True)
+    fwd_left = split_table(fwd, 1)
+    sent = [z_forward(coefficients, fwd_left, part, devices, width, zl) for part in range(2)]
+    first = lax.all_to_all(sent[0], "pencil", split_axis=0, concat_axis=0, tiled=True)
+    first, later = lax.optimization_barrier((first, sent[1]))
+    second = lax.all_to_all(later, "pencil", split_axis=0, concat_axis=0, tiled=True)
     z = point_offset // (GRID_SIDE * GRID_SIDE)
     y = point_offset // GRID_SIDE % GRID_SIDE
     x = point_offset % GRID_SIDE
-    points = (((z * 2 + y // 128) * 2 * GRID_SIDE + x) * 128 + y % 128).reshape(-1)
+    point_rows = (((z * 2 + y // 128) * GRID_SIDE + x) * 8).reshape(-1)
+    turn = y % 128 - jnp.arange(npts, dtype=jnp.int32) % 128
+    shifts_in = (-turn % 128).reshape(-1)
+    shifts_out = (turn % 128).reshape(-1)
     used = slot_count
-    field, picked = grid_and_gather(
-        pieces, split_table(fwd_x, 1), split_table(fwd.T, 0), points, used,
-        devices, width, zl, slots, npts,
-    )
     live = jnp.arange(slots, dtype=jnp.int32) < used[0]
-    coeffs = jnp.einsum("smt,spt->smp", picked, proj_value, precision=highest)
     coeff_width = 16 * NPROJ
-    coeffs = jnp.where(live[:, None, None], coeffs, 0.0).reshape(slots, coeff_width)
+    fields = []
+    parts = []
+    for pieces in (first, second):
+        field, picked = grid_and_gather(
+            pieces, split_table(fwd_x, 1), split_table(fwd.T, 0), point_rows, shifts_in, used,
+            devices, width, zl, slots, npts,
+        )
+        fields.append(field)
+        picked = picked.reshape(slots, npts // 128, 8, 128)
+        values = proj_value.reshape(slots, NPROJ, npts // 128, 128)
+        part = jnp.einsum("shmt,spht->smp", picked, values, precision=highest)
+        parts.append(part.reshape(slots, 2, HALF, NPROJ))
+    coeffs = jnp.concatenate(parts, 2)
+    coeffs = jnp.where(live[:, None, None, None], coeffs, 0.0).reshape(slots, coeff_width)
     atom_dev = proj_strength.shape[0] // devices
     column_proj = jnp.arange(coeff_width, dtype=jnp.int32) % NPROJ
     window_size = 2 * REACH + 1
@@ -537,17 +547,29 @@
         ],
         0,
     )
-    energy = jnp.dot(onehot, window, precision=highest).reshape(slots, 16, NPROJ)
-    terms = jnp.einsum("smp,spt->smt", energy, proj_value, precision=highest)
+    energy = jnp.dot(onehot, window, precision=highest).reshape(slots, 2, 2, HALF, NPROJ)
     pot = potential.reshape(zl, 2, 128, GRID_SIDE).transpose(0, 1, 3, 2)
-    back = scatter_and_back(
-        field, pot, terms, split_table(bwd.T, 0), split_table(bwd_x, 1), points, used,
-        devices, width, zl,
-    )
-    pieces = lax.all_to_all(back, "pencil", split_axis=0, concat_axis=0, tiled=True)
-    applied_coefficients = z_backward(
-        pieces, split_table(bwd.T, 0), coefficients, device, devices, width, zl
-    )
+    bwd_right = split_table(bwd.T, 0)
+    backs = []
+    for part in range(2):
+        terms = jnp.einsum(
+            "smp,spt->smt", energy[:, :, part].reshape(slots, 8, NPROJ), proj_value, precision=highest
+        )
+        if part == 1:
+            backs[0], terms = lax.optimization_barrier((backs[0], terms))
+        back = scatter_and_back(
+            fields[part], pot, terms, bwd_right, split_table(bwd_x, 1), point_rows, shifts_out, used,
+            devices, width, zl,
+        )
+        backs.append(back)
+    backs = [
+        lax.all_to_all(back, "pencil", split_axis=0, concat_axis=0, tiled=True) for back in backs
+    ]
+    applied_coefficients = None
+    for part in range(2):
+        applied_coefficients = z_backward(
+            backs[part], bwd_right, coefficients, applied_coefficients, part, device, devices, width, zl
+        )
     return (applied_coefficients, becp_home)
 
 

time: 789 us -> 654 us (0.83)
  blocking collectives: 303 us -> 0 us
  starting transfers between devices: 17.4 us -> 115 us
  waiting for transfers between devices: 190 us -> 242 us
  local copies, waits for them, and re-layouts: 11 us -> 29 us
    all_to_all x1 -> x0, blocking collectives: 303 us -> none  [per_device_fast(): lax.all_to_all(back, 'pencil', split_axis=0, concat_axis=0, tiled=True)]
    all_to_all x1 -> x4, starting transfers between devices: 7.43 us -> 89.2 us  [the longest x2 77.7 us: per_device_fast(): lax.all_to_all(back, 'pencil', split_axis=0, concat_axis=0, tiled=True)]
    all_to_all x1 -> x4, waiting for transfers between devices: 184 us -> 233 us  [the longest x2 102 us: per_device_fast(): lax.all_to_all(back, 'pencil', split_axis=0, concat_axis=0, tiled=True)]
    pallas_call x1 -> x2, Pallas kernels: 112 us -> 92.3 us  [grid_and_gather(): pl.pallas_call(body, grid=(bands,), in_specs=[pl.BlockSpec(memory_space=p...]
    pallas_call x1 -> x2, Pallas kernels: 127 us -> 146 us  [scatter_and_back(): pl.pallas_call(body, grid=(zl,), in_specs=[pl.BlockSpec(memory_space=pltp...]
    ppermute x8, starting transfers between devices: 9.94 us -> 26.3 us  [passed_along(): return lax.ppermute(block, axis, route)]
    unnamed x25 -> x51, local copies, waits for them, and re-layouts: 7.33 us -> 21.5 us
  transfers between devices with their start and end apart: 9 -> 12, of which waited for: 5 -> 8; matrix products, arithmetic and copies ran while one was open for 1% -> 1% of each run, Pallas kernels for 0% -> 20%
where the time goes in v2:
time: 654 us; the launch traced here: 655 us
  Pallas kernels  260 us (40%)
  waiting for transfers between devices  242 us (37%)
  starting transfers between devices  115 us (18%)
  local copies, waits for them, and re-layouts  29 us (4%)
  matrix products  6.99 us (1%)
    pallas_call x2, Pallas kernels, scatter_and_back(): pl.pallas_call(body, grid=(zl,), in_specs=[pl.BlockSpec(memory_space=pltp...  146 us
    all_to_all x2, waiting for transfers between devices, per_device_fast(): lax.all_to_all(back, 'pencil', split_axis=0, concat_axis=0, tiled=True)  102 us
    pallas_call x2, Pallas kernels, grid_and_gather(): pl.pallas_call(body, grid=(bands,), in_specs=[pl.BlockSpec(memory_space=p...  92.3 us
    all_to_all x1, waiting for transfers between devices, per_device_fast(): lax.all_to_all(sent[0], 'pencil', split_axis=0, concat_axis=0, tiled=True)  86.8 us
    all_to_all x2, starting transfers between devices, per_device_fast(): lax.all_to_all(back, 'pencil', split_axis=0, concat_axis=0, tiled=True)  77.7 us
    all_to_all x1, waiting for transfers between devices, per_device_fast(): lax.all_to_all(later, 'pencil', split_axis=0, concat_axis=0, tiled=True)  45.1 us
    ppermute x8, starting transfers between devices, passed_along(): return lax.ppermute(block, axis, route)  26.3 us
    unnamed x51, local copies, waits for them, and re-layouts  21.5 us
  transfers between devices with their start and end apart: 12, of which 8 were waited for; matrix products, arithmetic and copies ran while one was open for 1% of the time, Pallas kernels for 20%

profile of v2, /device:TPU:0, one launch (start us, length us, event | category | flops | bytes accessed | tf_op | source)
XLA Modules:
  0.0 655.4 jit_solution(567674786255166208)
XLA Ops:
  0.7 2.2 copy-done.2
  2.9 1.1 copy-done.17
  4.0 2.9 z_forward.2
  6.9 2.0 copy-done.9
  8.9 7.4 %all-to-all-start = ((f32[32,4,2,4,8,128]{5,4,3,2,1,0:T(8,128)}), f32[32,4,2,4,8,128]{5,4,3,2,1,0:T(8,128)}, u32[]{:S(2)}, u32[]{:S(2)}) async-start(f32[32,4,2,4,8,128]{5,4,3,2,1,0:T(8,128)} %copy-done.9), calls=%async_computation | async-start | bytes 8388608 | tf_op jit(solution)/shard_map/all_to_all | solution.py:494
  16.4 2.2 copy-done.3
  18.6 2.9 z_forward.3
  21.5 2.0 copy-done.6
  23.5 86.8 %all-to-all-done = f32[32,4,2,4,8,128]{5,4,3,2,1,0:T(8,128)} async-done(((f32[32,4,2,4,8,128]{5,4,3,2,1,0:T(8,128)}), f32[32,4,2,4,8,128]{5,4,3,2,1,0:T(8,128)}, u32[]{:S(2)}, u32[]{:S(2)}) %all-to-all-start) | async-done | bytes 4194336 | tf_op jit(solution)/shard_map/all_to_all | solution.py:494
  110.2 4.1 all-to-all-start.1
  115.3 0.8 constant_dynamic-slice_fusion
  116.2 46.2 %grid_and_gather.3 = (f32[32768,128]{1,0:T(8,128)}, f32[128,8,128]{2,1,0:T(8,128)S(1)}) custom-call(s32[16384]{0:T(1024)S(1)} %bitcast.52, s32[16384]{0:T(1024)S(1)} %bitcast.58, s32[1]{0:T(128)} %copy.38.used_ref, f32[32,4,64,128]{3,2,1,0:T(8,128)} %bitcast.4.r_ref, bf16[512,768]{1,0:T(8,128)(2,1)S(1)} %copy-done.15, bf16[768,512]{1,0:T(8,128)(2,1)S(1)} %copy-done.16), custom_call_target="tpu_custom_call" | custom-call | flops 12884901888 | bytes 201326592 | tf_op jit(solution)/shard_map/grid_and_gather/pallas_call | solution.py:328
  162.4 0.6 fusion.2
  163.1 45.1 %all-to-all-done.1 = f32[32,4,2,4,8,128]{5,4,3,2,1,0:T(8,128)} async-done(((f32[32,4,2,4,8,128]{5,4,3,2,1,0:T(8,128)}), f32[32,4,2,4,8,128]{5,4,3,2,1,0:T(8,128)}, u32[]{:S(2)}, u32[]{:S(2)}) %all-to-all-start.1) | async-done | bytes 4194336 | tf_op jit(solution)/shard_map/all_to_all | solution.py:496
  208.2 46.1 %grid_and_gather.2 = (f32[32768,128]{1,0:T(8,128)}, f32[128,8,128]{2,1,0:T(8,128)S(1)}) custom-call(s32[16384]{0:T(1024)S(1)} %bitcast.53, s32[16384]{0:T(1024)S(1)} %bitcast.59, s32[1]{0:T(128)} %copy.38.used_ref, f32[32,4,64,128]{3,2,1,0:T(8,128)} %bitcast.1.r_ref, bf16[512,768]{1,0:T(8,128)(2,1)S(1)} %copy-done.15, bf16[768,512]{1,0:T(8,128)(2,1)S(1)} %copy-done.16), custom_call_target="tpu_custom_call" | custom-call | flops 12884901888 | bytes 201326592 | tf_op jit(solution)/shard_map/grid_and_gather/pallas_call | solution.py:328
  254.4 0.6 fusion
  255.5 2.2 collective-permute-start
  257.7 16.6 %collective-permute-start.1 = (f32[16,128]{1,0:T(8,128)S(1)}, f32[16,128]{1,0:T(8,128)S(1)}, u32[]{:S(2)}, u32[]{:S(2)}) collective-permute-start(f32[16,128]{1,0:T(8,128)S(1)} %get-tuple-element.28), channel_id=1, source_target_pairs={{1,0},{2,1},{3,2},{4,3},{5,4},{6,5},{7,6},{8,7},{9,8},{10,9},{11,1... | collective-permute-start | bytes 24584 | tf_op jit(solution)/shard_map/ppermute | solution.py:21
  274.3 0.8 dynamic_slice.6
  275.1 0.5 collective-permute-done.1
  275.7 5.3 collective-permute-done.2
  281.0 0.6 collective-permute-done.3
  281.6 0.7 fusion.34
  282.3 1.9 copy.20
  284.3 5.3 collective-permute-start.6
  289.6 2.0 collective-permute-start.7
  291.7 1.6 collective-permute-done.7
  293.2 0.9 fusion.21
  294.1 0.6 fusion.36
  294.8 1.6 copy.25
  296.4 2.3 fusion.38.terms_ref
  298.7 1.6 copy.26
  300.3 2.3 fusion.39.terms_ref
  302.6 1.0 copy-done.12
  303.7 1.1 copy-done.13
  304.8 73.2 %scatter_and_back.2 = f32[32,8,32,128]{3,2,1,0:T(8,128)S(1)} custom-call(s32[16384]{0:T(1024)S(1)} %bitcast.54, s32[16384]{0:T(1024)S(1)} %bitcast.56, s32[1]{0:T(128)} %copy.38.used_ref, f32[32768,128]{1,0:T(8,128)} %get-tuple-element.13.u_ref, f32[8,2,256,128]{3,2,1,0:T(8,128)S(1)} %bitcast.48, f32[64,8,256]{2,1,0:T(8,128)S(1)} %copy-done.12, ...), custom_call_target="tpu_custom_call" | custom-call | flops 12884901888 | bytes 268435456 | tf_op jit(solution)/shard_map/scatter_and_back/pallas_call | solution.py:405
  378.0 2.0 copy-done.8
  380.0 45.6 %all-to-all-start.3 = ((f32[32,8,32,128]{3,2,1,0:T(8,128)}), f32[32,8,32,128]{3,2,1,0:T(8,128)}, u32[]{:S(2)}, u32[]{:S(2)}) async-start(f32[32,8,32,128]{3,2,1,0:T(8,128)} %copy-done.8), calls=%async_computation.3 | async-start | bytes 8388608 | tf_op jit(solution)/shard_map/all_to_all | solution.py:566
  425.6 1.1 copy-done.14
  426.7 73.2 %scatter_and_back.3 = f32[32,8,32,128]{3,2,1,0:T(8,128)S(1)} custom-call(s32[16384]{0:T(1024)S(1)} %bitcast.55, s32[16384]{0:T(1024)S(1)} %bitcast.57, s32[1]{0:T(128)} %copy.38.used_ref, f32[32768,128]{1,0:T(8,128)} %get-tuple-element.11.u_ref, f32[8,2,256,128]{3,2,1,0:T(8,128)S(1)} %bitcast.49, f32[64,8,256]{2,1,0:T(8,128)S(1)} %copy-done.11, ...), custom_call_target="tpu_custom_call" | custom-call | flops 12884901888 | bytes 268435456 | tf_op jit(solution)/shard_map/scatter_and_back/pallas_call | solution.py:405
  499.9 2.0 copy-done.7
  501.9 17.6 %all-to-all-done.3 = f32[32,8,32,128]{3,2,1,0:T(8,128)} async-done(((f32[32,8,32,128]{3,2,1,0:T(8,128)}), f32[32,8,32,128]{3,2,1,0:T(8,128)}, u32[]{:S(2)}, u32[]{:S(2)}) %all-to-all-start.3) | async-done | bytes 4194336 | tf_op jit(solution)/shard_map/all_to_all | solution.py:566
  519.5 32.1 %all-to-all-start.2 = ((f32[32,8,32,128]{3,2,1,0:T(8,128)}), f32[32,8,32,128]{3,2,1,0:T(8,128)}, u32[]{:S(2)}, u32[]{:S(2)}) async-start(f32[32,8,32,128]{3,2,1,0:T(8,128)} %copy-done.7), calls=%async_computation.2 | async-start | bytes 8388608 | tf_op jit(solution)/shard_map/all_to_all | solution.py:566
  551.6 2.2 copy-done.4
  553.8 7.7 %z_backward.2.rest_0_ = f32[2,8,512,128]{3,2,1,0:T(8,128)} custom-call(s32[1]{0:T(128)} %bitcast.dev_ref, f32[8192,128]{1,0:T(8,128)} %bitcast.21.r_ref, bf16[1536,256]{1,0:T(8,128)(2,1)S(1)} %copy-done.10, f32[2,8,512,128]{3,2,1,0:T(8,128)S(1)} %copy-done.4), custom_call_target="tpu_custom_call" | custom-call | flops 3221225472 | bytes 25165824 | tf_op jit(solution)/shard_map/z_backward/pallas_call | solution.py:462
  561.4 84.0 %all-to-all-done.2 = f32[32,8,32,128]{3,2,1,0:T(8,128)} async-done(((f32[32,8,32,128]{3,2,1,0:T(8,128)}), f32[32,8,32,128]{3,2,1,0:T(8,128)}, u32[]{:S(2)}, u32[]{:S(2)}) %all-to-all-start.2) | async-done | bytes 4194336 | tf_op jit(solution)/shard_map/all_to_all | solution.py:566
  645.5 2.2 copy-done.5
  647.7 7.7 %z_backward.3 = f32[2,8,512,128]{3,2,1,0:T(8,128)} custom-call(s32[1]{0:T(128)} %bitcast.dev_ref, f32[8192,128]{1,0:T(8,128)} %bitcast.20.r_ref, bf16[1536,256]{1,0:T(8,128)(2,1)S(1)} %copy-done.10, f32[2,8,512,128]{3,2,1,0:T(8,128)S(1)} %copy-done.5, f32[2,8,512,128]{3,2,1,0:T(8,128)} %z_backward.2.rest_0_), custom_call_target="tpu_custom_call", output_to_operand_aliasing={{}: (4, {})} | custom-call | flops 3221225472 | bytes 25165824 | tf_op jit(solution)/shard_map/z_backward/pallas_call | solution.py:462
  (61 shorter events, 1.2 us)
Async XLA Ops:
  0.6 161.7 %copy-start = (f32[64,8,256]{2,1,0:T(8,128)S(1)}, f32[64,8,256]{2,1,0:T(8,128)}, u32[]{:S(2)}) copy-start(f32[64,8,256]{2,1,0:T(8,128)} %param.21) | copy-start | bytes 1572868
  0.6 2.2 copy-start.2
  2.9 1.1 copy-start.17
  6.9 2.0 copy-start.9
  8.9 7.4 %copy-start.18 = (bf16[512,768]{1,0:T(8,128)(2,1)S(1)}, bf16[512,768]{1,0:T(8,128)(2,1)}, u32[]{:S(2)}) copy-start(bf16[512,768]{1,0:T(8,128)(2,1)} %constant.156.clone.t_ref) | copy-start | bytes 2359300
  8.9 101.3 %all-to-all-start = ((f32[32,4,2,4,8,128]{5,4,3,2,1,0:T(8,128)}), f32[32,4,2,4,8,128]{5,4,3,2,1,0:T(8,128)}, u32[]{:S(2)}, u32[]{:S(2)}) async-start(f32[32,4,2,4,8,128]{5,4,3,2,1,0:T(8,128)} %copy-done.9), calls=%async_computation | async-start | bytes 8388608 | tf_op jit(solution)/shard_map/all_to_all | solution.py:494
  16.4 2.2 copy-start.3
  21.4 2.0 copy-start.6
  23.5 90.9 %copy-start.19 = (s32[64,256]{1,0:T(8,128)S(1)}, s32[64,256]{1,0:T(8,128)}, u32[]{:S(2)}) copy-start(s32[64,256]{1,0:T(8,128)} %param.20) | copy-start | bytes 196612
  23.5 92.7 %copy-start.21 = (s32[64]{0:T(128)S(1)}, s32[64]{0:T(128)}, u32[]{:S(2)}) copy-start(s32[64]{0:T(128)} %param.18) | copy-start | bytes 772
  23.5 92.7 %copy-start.15 = (bf16[512,768]{1,0:T(8,128)(2,1)S(1)}, bf16[512,768]{1,0:T(8,128)(2,1)}, u32[]{:S(2)}) copy-start(bf16[512,768]{1,0:T(8,128)(2,1)} %constant.157.clone.x_ref) | copy-start | bytes 2359300
  23.5 92.7 %copy-start.16 = (bf16[768,512]{1,0:T(8,128)(2,1)S(1)}, bf16[768,512]{1,0:T(8,128)(2,1)}, u32[]{:S(2)}) copy-start(bf16[768,512]{1,0:T(8,128)(2,1)} %constant.158.clone.y_ref) | copy-start | bytes 2359300
  110.2 98.0 %all-to-all-start.1 = ((f32[32,4,2,4,8,128]{5,4,3,2,1,0:T(8,128)}), f32[32,4,2,4,8,128]{5,4,3,2,1,0:T(8,128)}, u32[]{:S(2)}, u32[]{:S(2)}) async-start(f32[32,4,2,4,8,128]{5,4,3,2,1,0:T(8,128)} %copy-done.6), calls=%async_computation.1 | async-start | bytes 8388608 | tf_op jit(solution)/shard_map/all_to_all | solution.py:496
  116.1 139.0 %copy-start.20 = (s32[64]{0:T(128)}, s32[64]{0:T(128)S(1)}, u32[]{:S(2)}) copy-start(s32[64]{0:T(128)S(1)} %fusion.31) | copy-start | bytes 772
  255.1 47.5 %copy-start.10 = (bf16[1536,256]{1,0:T(8,128)(2,1)S(1)}, bf16[1536,256]{1,0:T(8,128)(2,1)}, u32[]{:S(2)}) copy-start(bf16[1536,256]{1,0:T(8,128)(2,1)} %constant.159.clone.y_ref.t_ref) | copy-start | bytes 2359300
  255.5 19.7 %collective-permute-start = (f32[16,128]{1,0:T(8,128)S(1)}, f32[16,128]{1,0:T(8,128)S(1)}, u32[]{:S(2)}, u32[]{:S(2)}) collective-permute-start(f32[16,128]{1,0:T(8,128)S(1)} %get-tuple-element.25), channel_id=1, source_target_pairs={{2,0},{3,1},{4,2},{5,3},{6,4},{7,5},{8,6},{9,7},{10,8},{11,9},{12,... | collective-permute-start | bytes 24584 | tf_op jit(solution)/shard_map/ppermute | solution.py:21
  257.7 18.0 %collective-permute-start.1 = (f32[16,128]{1,0:T(8,128)S(1)}, f32[16,128]{1,0:T(8,128)S(1)}, u32[]{:S(2)}, u32[]{:S(2)}) collective-permute-start(f32[16,128]{1,0:T(8,128)S(1)} %get-tuple-element.28), channel_id=1, source_target_pairs={{1,0},{2,1},{3,2},{4,3},{5,4},{6,5},{7,6},{8,7},{9,8},{10,9},{11,1... | collective-permute-start | bytes 24584 | tf_op jit(solution)/shard_map/ppermute | solution.py:21
  274.3 6.7 %collective-permute-start.2 = (f32[16,128]{1,0:T(8,128)S(1)}, f32[16,128]{1,0:T(8,128)S(1)}, u32[]{:S(2)}, u32[]{:S(2)}) collective-permute-start(f32[16,128]{1,0:T(8,128)S(1)} %get-tuple-element.27), channel_id=1, source_target_pairs={{31,0},{0,1},{1,2},{2,3},{3,4},{4,5},{5,6},{6,7},{7,8},{8,9},{9,10... | collective-permute-start | bytes 24584 | tf_op jit(solution)/shard_map/ppermute | solution.py:21
  274.3 7.3 %collective-permute-start.3 = (f32[16,128]{1,0:T(8,128)S(1)}, f32[16,128]{1,0:T(8,128)S(1)}, u32[]{:S(2)}, u32[]{:S(2)}) collective-permute-start(f32[16,128]{1,0:T(8,128)S(1)} %get-tuple-element.26), channel_id=1, source_target_pairs={{30,0},{31,1},{0,2},{1,3},{2,4},{3,5},{4,6},{5,7},{6,8},{7,9},{8,1... | collective-permute-start | bytes 24584 | tf_op jit(solution)/shard_map/ppermute | solution.py:21
  282.2 9.4 %collective-permute-start.4 = (f32[16,128]{1,0:T(8,128)S(1)}, f32[16,128]{1,0:T(8,128)S(1)}, u32[]{:S(2)}, u32[]{:S(2)}) collective-permute-start(f32[16,128]{1,0:T(8,128)S(1)} %get-tuple-element.18), channel_id=1, source_target_pairs={{30,0},{31,1},{0,2},{1,3},{2,4},{3,5},{4,6},{5,7},{6,8},{7,9},{8,1... | collective-permute-start | bytes 24584 | tf_op jit(solution)/shard_map/ppermute | solution.py:21
  284.2 7.4 %collective-permute-start.5 = (f32[16,128]{1,0:T(8,128)S(1)}, f32[16,128]{1,0:T(8,128)S(1)}, u32[]{:S(2)}, u32[]{:S(2)}) collective-permute-start(f32[16,128]{1,0:T(8,128)S(1)} %get-tuple-element.18), channel_id=1, source_target_pairs={{31,0},{0,1},{1,2},{2,3},{3,4},{4,5},{5,6},{6,7},{7,8},{8,9},{9,10... | collective-permute-start | bytes 24584 | tf_op jit(solution)/shard_map/ppermute | solution.py:21
  284.3 7.4 %collective-permute-start.6 = (f32[16,128]{1,0:T(8,128)S(1)}, f32[16,128]{1,0:T(8,128)S(1)}, u32[]{:S(2)}, u32[]{:S(2)}) collective-permute-start(f32[16,128]{1,0:T(8,128)S(1)} %get-tuple-element.18), channel_id=1, source_target_pairs={{1,0},{2,1},{3,2},{4,3},{5,4},{6,5},{7,6},{8,7},{9,8},{10,9},{11,1... | collective-permute-start | bytes 24584 | tf_op jit(solution)/shard_map/ppermute | solution.py:21
  289.6 3.7 collective-permute-start.7
  302.6 1.0 copy-start.12
  303.7 1.1 copy-start.13
  378.0 2.0 copy-start.8
  380.0 45.6 %copy-start.11 = (f32[64,8,256]{2,1,0:T(8,128)S(1)}, f32[64,8,256]{2,1,0:T(8,128)}, u32[]{:S(2)}) copy-start(f32[64,8,256]{2,1,0:T(8,128)} %fusion.39.terms_ref) | copy-start | bytes 1572868
  380.0 139.5 %all-to-all-start.3 = ((f32[32,8,32,128]{3,2,1,0:T(8,128)}), f32[32,8,32,128]{3,2,1,0:T(8,128)}, u32[]{:S(2)}, u32[]{:S(2)}) async-start(f32[32,8,32,128]{3,2,1,0:T(8,128)} %copy-done.8), calls=%async_computation.3 | async-start | bytes 8388608 | tf_op jit(solution)/shard_map/all_to_all | solution.py:566
  425.6 1.1 copy-start.14
  499.9 2.0 copy-start.7
  519.5 126.0 %all-to-all-start.2 = ((f32[32,8,32,128]{3,2,1,0:T(8,128)}), f32[32,8,32,128]{3,2,1,0:T(8,128)}, u32[]{:S(2)}, u32[]{:S(2)}) async-start(f32[32,8,32,128]{3,2,1,0:T(8,128)} %copy-done.7), calls=%async_computation.2 | async-start | bytes 8388608 | tf_op jit(solution)/shard_map/all_to_all | solution.py:566
  551.6 2.2 copy-start.4
  645.5 2.2 copy-start.5
  647.7 7.7 %copy-start.1 = (f32[64,8,256]{2,1,0:T(8,128)S(1)}, f32[64,8,256]{2,1,0:T(8,128)}, u32[]{:S(2)}) copy-start(f32[64,8,256]{2,1,0:T(8,128)} %param.21) | copy-start | bytes 1572868
